TPU v7x, 512 devices: a whole 4x4x16 slice. The times are simulated.
512 devices in a mesh: rep: 8 (over y, x_lo), fsdp: 64 (over x_hi, z, core).
Axes of the slice: x: 4 (x_hi: 2, x_lo: 2; x = x_hi * 2 + x_lo), y: 4, z: 16, core: 2. Of those that a mesh axis runs over, the one named last changes fastest.
Arguments:
- x_in: bfloat16 [8, 8192, 512], P('rep', 'fsdp'), may hold values from -16 to 16
- d_out: bfloat16 [8, 8192, 512], P('rep', 'fsdp'), may hold values from -0.375 to 0.375
- gate_weight: bfloat16 [64, 128, 128], P('fsdp'), may hold values from -0.25 to 0.25
- up_weight: bfloat16 [64, 128, 128], P('fsdp'), may hold values from -0.25 to 0.25
- down_weight: bfloat16 [64, 128, 128], P('fsdp'), may hold values from -0.125 to 0.125
- mom_gate: float32 [8, 64, 128, 128], P('rep', 'fsdp'), may hold values from -6 to 6
- mom_up: float32 [8, 64, 128, 128], P('rep', 'fsdp'), may hold values from -6 to 6
- mom_down: float32 [8, 64, 128, 128], P('rep', 'fsdp'), may hold values from -6 to 6
- band_index: int32 [3, 64, 512], P(None, 'fsdp'), may hold values from 0 to 16383, as said below
Outputs:
- res_gate: float32 [8, 64, 128, 128], P('rep', 'fsdp')
- res_up: float32 [8, 64, 128, 128], P('rep', 'fsdp')
- down_residual_blocks: float32 [8, 64, 128, 128], P('rep', 'fsdp')
- upd_gate: float32 [64, 128, 128], P('fsdp')
- upd_up: float32 [64, 128, 128], P('fsdp')
- upd_down: float32 [64, 128, 128], P('fsdp')
Inputs may be any that keep to these rules, and one draw needn't show every extreme that they name: `band_index`: each row of 512 positions of a block holds distinct values; the positions are the same for every replica group.
All inputs are finite; a program needn't handle non-finite values.
Results may differ from a plain program's by a relative error of at most 0.0028.
Values may be sent and summed in bfloat16 or wider, within the bound.
A program may use at most 128 MiB of HBM per device.

v0:
```python
import jax
import jax.numpy as jnp
from jax import lax
from jax.sharding import PartitionSpec as P

momentum_decay = 0.999


def dct_table(side_len):
    freq_rows = jnp.arange(side_len, dtype=jnp.float32)[:, None]
    cell_cols = jnp.arange(side_len, dtype=jnp.float32)[None, :]
    weights = jnp.where(freq_rows == 0, jnp.sqrt(1.0 / side_len), jnp.sqrt(2.0 / side_len))
    return weights * jnp.cos(jnp.pi * (2.0 * cell_cols + 1.0) * freq_rows / (2.0 * side_len))


def forward_blocks(cosines, blocks):
    inner = jnp.matmul(cosines, blocks, precision=lax.Precision.HIGHEST)
    return jnp.matmul(inner, cosines.T, precision=lax.Precision.HIGHEST)


def inverse_blocks(cosines, coeffs):
    inner = jnp.matmul(cosines.T, coeffs, precision=lax.Precision.HIGHEST)
    return jnp.matmul(inner, cosines, precision=lax.Precision.HIGHEST)


def place_band(values, positions, side_len):
    layout = (positions.shape[0], positions.shape[1], side_len * side_len)
    matrix_ids = jnp.arange(layout[0])[:, None, None]
    span_ids = jnp.arange(layout[1])[None, :, None]
    filled = jnp.zeros(layout, values.dtype).at[matrix_ids, span_ids, positions].set(values)
    return filled.reshape(layout[0], layout[1], side_len, side_len)


def band_split(moments, gradients, band_index):
    side_len = moments.shape[2]
    updated = momentum_decay * moments + gradients
    cosines = dct_table(side_len)
    coeffs = forward_blocks(cosines, updated)
    flattened = coeffs.reshape(coeffs.shape[0], coeffs.shape[1], side_len * side_len)
    picked = jnp.take_along_axis(flattened, band_index, axis=2)
    kept_part = inverse_blocks(cosines, place_band(picked, band_index, side_len))
    return (updated - kept_part, picked)


def per_device(
    x_in, d_out, gate_weight, up_weight, down_weight, mom_gate, mom_up, mom_down, band_index
):
    x_rows = x_in[0]
    d_rows = d_out[0]
    span_side = gate_weight.shape[1]
    blk_dev = gate_weight.shape[0]
    tok_rows = x_rows.shape[0]
    shard_count = lax.axis_size("fsdp")
    row_blocks = x_rows.shape[1] // span_side
    col_blocks = blk_dev * shard_count // row_blocks
    input_row_blocks = x_rows.reshape(tok_rows, row_blocks, span_side)
    d_blocks = d_rows.reshape(tok_rows, row_blocks, span_side)
    col_parts = jnp.stack([input_row_blocks, d_blocks], axis=2)
    col_send = jnp.tile(col_parts, (1, col_blocks, 1, 1)).reshape(
        tok_rows, shard_count, blk_dev, col_parts.shape[2], span_side
    )
    col_ids_all = jnp.arange(col_blocks, dtype=jnp.int32)
    matrix_pieces = (
        lax.all_gather(gate_weight, "fsdp", axis=0, tiled=True),
        lax.all_gather(up_weight, "fsdp", axis=0, tiled=True),
        lax.all_gather(down_weight, "fsdp", axis=0, tiled=True),
    )
    count = matrix_pieces[0].shape[0]
    block_ids = jnp.arange(count, dtype=jnp.int32)
    row_ids = block_ids % row_blocks
    column_numbers = block_ids // row_blocks
    x_sel = jnp.take(input_row_blocks, row_ids, axis=1)
    selected_delta = jnp.take(d_blocks, row_ids, axis=1)
    paired = jnp.concatenate([matrix_pieces[0], matrix_pieces[1]], axis=2)
    gu_terms = jnp.einsum("tic,ice->tie", x_sel, paired, preferred_element_type=jnp.float32)
    hidden_delta_terms = jnp.einsum(
        "bpd,pud->bpu", selected_delta, matrix_pieces[2], preferred_element_type=jnp.float32
    )
    placer = (column_numbers[:, None] == col_ids_all[None, :]).astype(jnp.float32)
    gu_new = jnp.einsum("tie,if->tfe", gu_terms, placer, precision=lax.Precision.HIGHEST)
    dh_new = jnp.einsum("tie,if->tfe", hidden_delta_terms, placer, precision=lax.Precision.HIGHEST)
    gate_pre = gu_new[:, :, :span_side]
    up_pre = gu_new[:, :, span_side:]
    sigmoid_gate = jax.nn.sigmoid(gate_pre)
    hidden = (gate_pre * sigmoid_gate * up_pre).astype(jnp.bfloat16)
    d_gate = (dh_new * up_pre * sigmoid_gate * (1.0 + gate_pre * (1.0 - sigmoid_gate))).astype(
        jnp.bfloat16
    )
    d_up = (dh_new * gate_pre * sigmoid_gate).astype(jnp.bfloat16)
    act_parts = jnp.stack([d_gate, d_up, hidden], axis=2)
    act_send = jnp.repeat(act_parts, row_blocks, axis=1).reshape(
        tok_rows, shard_count, blk_dev, act_parts.shape[2], span_side
    )
    matrix_pieces = (
        lax.all_to_all(col_send, "fsdp", split_axis=1, concat_axis=0, tiled=True),
        lax.all_to_all(act_send, "fsdp", split_axis=1, concat_axis=0, tiled=True),
    )
    cols = matrix_pieces[0][:, 0]
    acts = matrix_pieces[1][:, 0]
    g_gate = jnp.einsum(
        "tic,tid->icd", cols[:, :, 0], acts[:, :, 0], preferred_element_type=jnp.float32
    )
    g_up = jnp.einsum(
        "tic,tid->icd", cols[:, :, 0], acts[:, :, 1], preferred_element_type=jnp.float32
    )
    g_down = jnp.einsum(
        "tic,tid->icd", acts[:, :, 2], cols[:, :, 1], preferred_element_type=jnp.float32
    )
    moments = jnp.stack([mom_gate[0], mom_up[0], mom_down[0]])
    gradients = jnp.stack([g_gate, g_up, g_down])
    remains, picked = band_split(moments, gradients, band_index)
    summed = jnp.sum(lax.all_gather(picked[None], "rep", axis=0, tiled=True), axis=0)
    updates = inverse_blocks(dct_table(span_side), place_band(summed, band_index, span_side))
    return (
        remains[0][None],
        remains[1][None],
        remains[2][None],
        updates[0],
        updates[1],
        updates[2],
    )


def solution(mesh):
    in_specs = (
        P("rep", "fsdp", None),
        P("rep", "fsdp", None),
        P("fsdp", None, None),
        P("fsdp", None, None),
        P("fsdp", None, None),
        P("rep", "fsdp", None, None),
        P("rep", "fsdp", None, None),
        P("rep", "fsdp", None, None),
        P(None, "fsdp", None),
    )
    out_specs = (
        P("rep", "fsdp", None, None),
        P("rep", "fsdp", None, None),
        P("rep", "fsdp", None, None),
        P("fsdp", None, None),
        P("fsdp", None, None),
        P("fsdp", None, None),
    )
    return jax.shard_map(
        per_device, mesh=mesh, in_specs=in_specs, out_specs=out_specs, check_vma=False
    )
```

profile of v0, /device:TPU:1, one launch (start us, length us, event | category | flops | bytes accessed | tf_op | source)
XLA Modules:
  0.0 879.7 jit_solution(16766211450646183932)
XLA Ops:
  7.2 0.9 stack_reshape_squeeze.6
  8.1 0.9 stack_reshape_squeeze.7
  9.1 0.2 pad_maximum_fusion.1
  9.3 3.0 tile.8
  12.3 19.9 %all-to-all-start = ((bf16[128,64,1,2,128]{4,0,3,2,1:T(8,128)(2,1)}), bf16[128,64,1,2,128]{4,0,3,2,1:T(8,128)(2,1)}, u32[]{:S(2)}, u32[]{:S(2)}) async-start(bf16[128,64,1,2,128]{4,0,3,2,1:T(8,128)(2,1)} %bitcast.141), calls=%async_computation | async-start | bytes 8388608 | tf_op jit(solution)/shard_map/all_to_all | solution.py:95
  32.3 0.7 all-gather.7.cloned.1.call-update
  33.0 0.7 all-gather.9.cloned.1.call-update
  33.8 0.7 all-gather.5.cloned.1.call-update
  34.6 0.1 copy.37
  34.8 0.1 copy.43
  34.9 0.1 copy.38
  35.1 2.1 gather_fusion.2
  37.2 0.9 gather_fusion.1
  38.2 187.3 %all-gather.7.cloned.1.call-done = bf16[64,128,128]{2,1,0:T(8,128)(2,1)} async-done(((bf16[1,128,128]{2,1,0:T(8,128)(2,1)}), bf16[64,128,128]{2,1,0:T(8,128)(2,1)}) %all-gather.7.cloned.1.call-update) | async-done | bytes 2097168 | tf_op jit(solution)/shard_map/all_gather | solution.py:64
  225.4 4.1 copy.40
  229.5 141.6 %all-gather.9.cloned.1.call-done = bf16[64,128,128]{2,1,0:T(8,128)(2,1)} async-done(((bf16[1,128,128]{2,1,0:T(8,128)(2,1)}), bf16[64,128,128]{2,1,0:T(8,128)(2,1)}) %all-gather.9.cloned.1.call-update) | async-done | bytes 2097168 | tf_op jit(solution)/shard_map/all_gather | solution.py:65
  371.1 4.1 copy.41
  375.1 7.4 fusion.6
  382.6 9.2 %copy.44 = f32[128,64,256]{2,1,0:T(8,128)} copy(f32[128,64,256]{0,2,1:T(8,128)} %fusion.6) | data formatting | bytes 16777216 | tf_op jit(solution)/shard_map/tic,ice->tie/transpose | solution.py:75
  391.7 120.9 %all-gather.5.cloned.1.call-done = bf16[64,128,128]{2,1,0:T(8,128)(2,1)} async-done(((bf16[1,128,128]{2,1,0:T(8,128)(2,1)}), bf16[64,128,128]{2,1,0:T(8,128)(2,1)}) %all-gather.5.cloned.1.call-update) | async-done | bytes 2097168 | tf_op jit(solution)/shard_map/all_gather | solution.py:66
  512.6 3.4 convolution_bitcast_fusion
  516.0 0.6 copy-done
  516.6 2.8 convolution_bitcast_fusion.1
  519.5 4.4 fusion.28
  523.8 0.2 pad_maximum_fusion
  524.0 0.4 copy.45
  524.4 4.2 broadcast_in_dim.51
  528.7 8.2 all-to-all-start.1
  537.1 0.1 and_reduce_fusion
  537.3 4.7 copy.36
  542.0 271.2 %all-to-all-done.1 = bf16[128,64,1,3,128]{4,0,3,2,1:T(8,128)(2,1)} async-done(((bf16[128,64,1,3,128]{4,0,3,2,1:T(8,128)(2,1)}), bf16[128,64,1,3,128]{4,0,3,2,1:T(8,128)(2,1)}, u32[]{:S(2)}, u32[]{:S(2)}) %all-to-all-start.1) | async-done | bytes 6291488 | tf_op jit(solution)/shard_map/all_to_all | solution.py:96
  813.2 4.3 copy.46
  817.6 0.8 fusion.21
  818.3 0.8 fusion.22
  819.1 0.7 fusion.23
  820.0 0.6 convolution_bitcast_fusion.5
  820.6 0.6 convolution_bitcast_fusion.4
  821.1 0.1 copy.62
  821.3 13.4 %gather_fusion = f32[1536]{0:T(1024)S(1)} fusion(f32[3,16384]{1,0:T(4,128)S(1)} %bitcast.139, s32[1536]{0:T(1024)S(1)} %reshape.222), kind=kCustom, calls=%fused_computation.2 | custom fusion | bytes 24576 | tf_op jit(solution)/shard_map/jit(take_along_axis)/gather | solution.py:40
  834.8 22.1 %all-gather = f32[24,1,512]{2,1,0:T(1,128)S(1)} all-gather(f32[3,1,512]{2,1,0:T(1,128)S(1)} %get-tuple-element.8), channel_id=2, replica_groups=mesh['rep'=8,'fsdp'=64] {'rep'}, dimensions={0}, use_global_device_ids=true | all-gather | bytes 55296 | tf_op jit(solution)/shard_map/all_gather | solution.py:112
  857.0 6.3 scatter_custom_fusion.1
  863.3 0.6 convolution_bitcast_fusion.2
  863.9 0.6 fusion.35
  864.4 0.7 fusion.77
  865.1 6.3 scatter_custom_fusion
  871.4 0.6 convolution_bitcast_fusion.3
  872.0 0.6 convolution_subtract_fusion
  872.5 0.7 slice_bitcast_fusion.23
  (45 shorter events, 0.9 us)
Async XLA Ops:
  12.3 22.2 %copy-start.2 = (bf16[1,128,512]{2,1,0:T(8,128)(2,1)S(1)}, bf16[1,128,512]{2,1,0:T(8,128)(2,1)}, u32[]{:S(2)}) copy-start(bf16[1,128,512]{2,1,0:T(8,128)(2,1)} %param.11) | copy-start | bytes 393220
  12.3 22.3 %copy-start.3 = (bf16[1,128,512]{2,1,0:T(8,128)(2,1)S(1)}, bf16[1,128,512]{2,1,0:T(8,128)(2,1)}, u32[]{:S(2)}) copy-start(bf16[1,128,512]{2,1,0:T(8,128)(2,1)} %param.12) | copy-start | bytes 393220
  12.3 512.1 %all-to-all-start = ((bf16[128,64,1,2,128]{4,0,3,2,1:T(8,128)(2,1)}), bf16[128,64,1,2,128]{4,0,3,2,1:T(8,128)(2,1)}, u32[]{:S(2)}, u32[]{:S(2)}) async-start(bf16[128,64,1,2,128]{4,0,3,2,1:T(8,128)(2,1)} %bitcast.141), calls=%async_computation | async-start | bytes 8388608 | tf_op jit(solution)/shard_map/all_to_all | solution.py:95
  32.3 193.2 %all-gather.7.cloned.1.call-start = ((), (), s32[]{:S(2)}) async-start(), calls=%async_computation.3 | async-start | bytes 2129920 | tf_op jit(solution)/shard_map/all_gather | solution.py:64
  33.0 338.1 %all-gather.9.cloned.1.call-start = ((), (), s32[]{:S(2)}) async-start(), calls=%async_computation.4 | async-start | bytes 2129920 | tf_op jit(solution)/shard_map/all_gather | solution.py:65
  33.8 478.9 %all-gather.5.cloned.1.call-start = ((), (), s32[]{:S(2)}) async-start(), calls=%async_computation.2 | async-start | bytes 2129920 | tf_op jit(solution)/shard_map/all_gather | solution.py:66
  512.6 4.0 copy-start
  528.7 8.2 copy-start.7
  528.7 8.4 copy-start.8
  528.7 8.5 copy-start.9
  528.7 284.6 %all-to-all-start.1 = ((bf16[128,64,1,3,128]{4,0,3,2,1:T(8,128)(2,1)}), bf16[128,64,1,3,128]{4,0,3,2,1:T(8,128)(2,1)}, u32[]{:S(2)}, u32[]{:S(2)}) async-start(bf16[128,64,1,3,128]{4,0,3,2,1:T(8,128)(2,1)} %bitcast.140), calls=%async_computation.1 | async-start | bytes 12582912 | tf_op jit(solution)/shard_map/all_to_all | solution.py:96
  813.2 4.3 copy-start.1
  819.1 0.8 copy-start.4
  819.1 0.9 copy-start.5
  819.1 0.9 copy-start.6
Sparse Core Ops, SparseCore 0:
  36.4 188.9 all-gather.6
  228.7 142.3 all-gather.8
  374.4 138.2 all-gather.4
where the time goes:
time: 889 us; the launch traced here: 880 us
  waiting for transfers between devices  723 us (81%)
  local copies, waits for them, and re-layouts  67.9 us (8%)
  starting transfers between devices  28.2 us (3%)
  matrix products  23.6 us (3%)
  blocking collectives  22.1 us (2%)
  between operations  14.1 us (2%)
    all_to_all x1, waiting for transfers between devices, per_device(): lax.all_to_all(act_send, 'fsdp', split_axis=1, concat_axis=0, tiled=True)  271 us
    all_gather x1, waiting for transfers between devices, per_device(): lax.all_gather(gate_weight, 'fsdp', axis=0, tiled=True)  187 us
    all_gather x1, waiting for transfers between devices, per_device(): lax.all_gather(up_weight, 'fsdp', axis=0, tiled=True)  142 us
    all_gather x1, waiting for transfers between devices, per_device(): lax.all_gather(down_weight, 'fsdp', axis=0, tiled=True)  121 us
    all_gather x1, blocking collectives, per_device(): lax.all_gather(picked[None], 'rep', axis=0, tiled=True)  22.1 us
    all_to_all x1, starting transfers between devices, per_device(): lax.all_to_all(col_send, 'fsdp', split_axis=1, concat_axis=0, tiled=True)  19.9 us
  transfers between devices with their start and end apart: 5, of which 4 were waited for; matrix products, arithmetic and copies ran while one was open for 5% of the time, Pallas kernels for 0%

commit v1 on v0

v1 whole, which is shorter than its diff:
```python
import functools

import jax
import jax.numpy as jnp
import numpy as np
from jax import lax
from jax.experimental import pallas as pl
from jax.experimental.pallas import tpu as pltpu
from jax.sharding import PartitionSpec as P

MESH = pl.DeviceIdType.MESH
F32 = jnp.float32
BF16 = jnp.bfloat16
SIDE = 128
KEEP = 512
NZ = 16
QROWS = SIDE + 16


def dct_parts():
    k = np.arange(SIDE, dtype=np.float64)[:, None]
    n = np.arange(SIDE, dtype=np.float64)[None, :]
    s = np.where(k == 0, np.sqrt(1.0 / SIDE), np.sqrt(2.0 / SIDE))
    c = (s * np.cos(np.pi * (2.0 * n + 1.0) * k / (2.0 * SIDE))).astype(np.float32)
    out = []
    for t in (c, c.T):
        hi = t.astype(jnp.bfloat16)
        lo = (t - hi.astype(np.float32)).astype(jnp.bfloat16)
        out += [hi, lo]
    return np.stack(out)


def mm(a, b, dims):
    return lax.dot_general(a, b, (dims, ((), ())), preferred_element_type=F32)


NN = ((1,), (0,))
NT = ((1,), (1,))
TN = ((0,), (0,))


def split(a):
    hi = a.astype(BF16)
    return hi, (a - hi.astype(F32)).astype(BF16)


def mm3(a, b, dims):
    return mm(a[0], b[0], dims) + (mm(a[0], b[1], dims) + mm(a[1], b[0], dims))


def quantize(value, dst):
    top = jnp.maximum(jnp.max(jnp.abs(value), axis=0, keepdims=True), 1e-30)
    power = jnp.ceil(jnp.log2(top))
    steps = jnp.round(value * jnp.exp2(14.0 - power))
    dst[0:SIDE, :] = steps.astype(jnp.int32).astype(jnp.int16)
    dst[SIDE:QROWS, :] = jnp.broadcast_to(power.astype(jnp.int32), (16, SIDE)).astype(jnp.int16)


def restore(src):
    steps = src[0:SIDE, :].astype(jnp.int32).astype(F32)
    power = src[SIDE:QROWS, :].astype(jnp.int32).astype(F32)[0:1, :]
    return steps * jnp.exp2(power - 14.0)


def kernel(
    x_ref, d_ref, wg_ref, wu_ref, wd_ref, mg_ref, mu_ref, md_ref, band_ref, table_ref,
    rg_out, ru_out, rd_out, ug_out, uu_out, ud_out,
    tok_x, tok_d, wts, part, recv, send, fin, own, mom, band, table, pick_r, pick_c, vals, vals_all,
    load_sem, tok_send, tok_recv, sib_sem, ag_send, ag_recv, rs_send, rs_recv, fin_recv, own_sem,
    rep_send, rep_recv,
):
    f = lax.axis_index("fsdp")
    r = lax.axis_index("rep")
    core = f % 2
    z = (f // 2) % NZ
    xh = f // (2 * NZ)
    kz = z // 2
    sib = f + 1 - 2 * core
    partner = (1 - xh) * (2 * NZ) + z * 2 + core
    up = (z + 1) % NZ
    down = (z + NZ - 1) % NZ
    base = xh * (2 * NZ)
    up_same = base + up * 2 + core
    down_same = base + down * 2 + core
    own_rb = f % 4
    sib_rb = sib % 4
    own_kk = z // 4
    matched = (kz % 2) == core

    def remote(src, dst, ssem, rsem, target):
        return pltpu.make_async_remote_copy(
            src_ref=src, dst_ref=dst, send_sem=ssem, recv_sem=rsem,
            device_id={"fsdp": target}, device_id_type=MESH,
        )

    loads = [
        pltpu.make_async_copy(x_ref.at[0], tok_x.at[2 * xh + core], load_sem.at[0]),
        pltpu.make_async_copy(d_ref.at[0], tok_d.at[2 * xh + core], load_sem.at[1]),
        pltpu.make_async_copy(mg_ref.at[0, 0], mom.at[0], load_sem.at[2]),
        pltpu.make_async_copy(mu_ref.at[0, 0], mom.at[1], load_sem.at[3]),
        pltpu.make_async_copy(md_ref.at[0, 0], mom.at[2], load_sem.at[4]),
        pltpu.make_async_copy(band_ref, band, load_sem.at[5]),
        pltpu.make_async_copy(table_ref, table, load_sem.at[6]),
    ]
    w_loads = [
        pltpu.make_async_copy(w.at[0], wts.at[own_kk, own_rb, m], load_sem.at[7 + m])
        for m, w in enumerate((wg_ref, wu_ref, wd_ref))
    ]

    @pl.when(matched)
    def _():
        for c in w_loads:
            c.start()
    for c in loads:
        c.start()

    barrier = pltpu.get_barrier_semaphore()
    others = [sib, partner] + [base + zz * 2 + c for zz in (up, down) for c in (0, 1)]
    for t in others:
        pl.semaphore_signal(barrier, inc=1, device_id={"fsdp": t}, device_id_type=MESH)
    for i in range(1, 8):
        pl.semaphore_signal(barrier, inc=1, device_id={"rep": (r + i) % 8}, device_id_type=MESH)
    pl.semaphore_wait(barrier, len(others) + 7)

    w_sib = [
        remote(w.at[0], wts.at[own_kk, own_rb, m], sib_sem.at[0, m], sib_sem.at[1, m], sib)
        for m, w in enumerate((wg_ref, wu_ref, wd_ref))
    ]

    @pl.when(jnp.logical_not(matched))
    def _():
        for c in w_sib:
            c.start()

    mine = 2 * xh + core
    theirs = 2 * (1 - xh) + core
    tok_copies = []
    for i, (src, dst) in enumerate(((x_ref, tok_x), (d_ref, tok_d))):
        tok_copies.append(remote(src.at[0], dst.at[mine], tok_send.at[0, i], tok_recv.at[0, i], partner))
    for i, (src, dst) in enumerate(((x_ref, tok_x), (d_ref, tok_d))):
        tok_copies.append(remote(src.at[0], dst.at[mine], tok_send.at[1, i], tok_recv.at[1, i], sib))
    for c in tok_copies:
        c.start()
    forwards = [
        remote(dst.at[theirs], dst.at[theirs], tok_send.at[2, i], tok_recv.at[2, i], sib)
        for i, dst in enumerate((tok_x, tok_d))
    ]

    @pl.when(matched)
    def _():
        for m in range(3):
            w_loads[m].wait()
            w_sib[m].wait_recv()

    @pl.when(jnp.logical_not(matched))
    def _():
        for m in range(3):
            w_sib[m].wait_send()

    def ag_chunk(way, s):
        src = (z + NZ - s) % NZ if way == 0 else (z + s) % NZ
        return (src // 2) % 2 == core, src // 4, (src % 2) * 2

    def ag_copy(way, s, kk, rb0, j):
        rb = rb0 + j // 3
        piece = wts.at[kk, rb, j % 3]
        return remote(
            piece, piece, ag_send.at[way, s, j], ag_recv.at[way, s, j], up_same if way == 0 else down_same
        )

    def ag_step(s, carry):
        for way in (0, 1):
            last = 8 - way
            active, kk, rb0 = ag_chunk(way, s)

            @pl.when(jnp.logical_and(active, s <= last))
            def _():
                for j in range(6):
                    @pl.when(s > 0)
                    def _():
                        ag_copy(way, s - 1, kk, rb0, j).wait_recv()

                    @pl.when(s < last)
                    def _():
                        ag_copy(way, s, kk, rb0, j).start()
        return carry

    lax.fori_loop(0, 9, ag_step, 0)

    for c in tok_copies[:2]:
        c.wait_recv()
    for c in forwards:
        c.start()
    for c in loads:
        c.wait()

    spots = lax.broadcasted_iota(jnp.int32, (SIDE, KEEP), 0)
    for m in range(3):
        at = band[m]
        pick_r[m] = jnp.where(spots == lax.shift_right_logical(at, 7), 1.0, 0.0).astype(BF16)
        pick_c[m] = jnp.where(spots == lax.bitwise_and(at, 127), 1.0, 0.0).astype(BF16)
    vals[...] = jnp.zeros((8, KEEP), F32)
    recv[:, 0] = jnp.zeros((2, 3, 2, QROWS, SIDE), jnp.int16)

    for c in tok_copies[2:]:
        c.wait_recv()
    for c in forwards:
        c.wait_recv()

    def column(kk):
        xs = tok_x[...].reshape(4 * SIDE, 4 * SIDE)
        ds = tok_d[...].reshape(4 * SIDE, 4 * SIDE)
        w_gu = jnp.concatenate(
            [wts[kk, :, 0].reshape(4 * SIDE, SIDE), wts[kk, :, 1].reshape(4 * SIDE, SIDE)], axis=1
        )
        w_d = jnp.concatenate([wts[kk, i, 2] for i in range(4)], axis=1)
        gu = mm(xs, w_gu, NN)
        dh = mm(ds, w_d, NT)
        gate = gu[:, :SIDE]
        upp = gu[:, SIDE:]
        sg = jax.nn.sigmoid(gate)
        act = gate * sg
        hidden = (act * upp).astype(BF16)
        d_gate = (dh * upp * sg * (1.0 + gate * (1.0 - sg))).astype(BF16)
        d_up = (dh * act).astype(BF16)
        g_in = mm(xs, jnp.concatenate([d_gate, d_up], axis=1), TN)
        g_out = mm(hidden, ds, TN)
        for i in range(4):
            part[kk, i, 0] = g_in[i * SIDE:(i + 1) * SIDE, :SIDE]
            part[kk, i, 1] = g_in[i * SIDE:(i + 1) * SIDE, SIDE:]
            part[kk, i, 2] = g_out[:, i * SIDE:(i + 1) * SIDE]

    def rs_chunk(way, s):
        dest = (z + 8 - s) % NZ if way == 0 else (z + 9 + s) % NZ
        return (dest // 2) % 2 == core, dest // 4, (dest % 2) * 2

    def rs_copy(way, s, m):
        return remote(
            send.at[way, s, m], recv.at[way, s + 1, m], rs_send.at[way, s, m, 0], rs_recv.at[way, s + 1, m],
            up_same if way == 0 else down_same,
        )

    def fin_copy(way, s, m, c):
        to = base + (up if way == 0 else down) * 2 + c
        return remote(
            send.at[way, s, m, c], fin.at[way, m], rs_send.at[way, s, m, c], fin_recv.at[way, m], to
        )

    own_copy = remote(part.at[own_kk, sib_rb], own, own_sem.at[0], own_sem.at[1], sib)

    def rs_step(t, carry):
        s = t - 1

        @pl.when(s >= 0)
        def _():
            for way in (0, 1):
                steps = 8 - way
                active, kk, rb0 = rs_chunk(way, s)

                @pl.when(jnp.logical_and(active, s < steps))
                def _():
                    for m in range(3):
                        @pl.when(s > 0)
                        def _():
                            rs_copy(way, s - 1, m).wait_recv()
                        for c in range(2):
                            total = part[kk, rb0 + c, m] + restore(recv.at[way, s, m, c])
                            quantize(total, send.at[way, s, m, c])

                        @pl.when(s < steps - 1)
                        def _():
                            rs_copy(way, s, m).start()

                        @pl.when(s == steps - 1)
                        def _():
                            for c in range(2):
                                fin_copy(way, s, m, c).start()

        @pl.when(t < 4)
        def _():
            off_m = jnp.where(t == 0, 4, jnp.where(t == 1, 2, jnp.where(t == 2, 6, 0)))
            off_u = jnp.where(t == 0, 5, jnp.where(t == 1, 3, jnp.where(t == 2, 1, 7)))
            k = (kz + jnp.where(matched, off_m, off_u)) % 8
            column(k // 2)

        @pl.when(jnp.logical_and(t == 3, matched))
        def _():
            own_copy.start()
            own[...] = part[own_kk, own_rb]
        return carry

    lax.fori_loop(0, 9, rs_step, 0)

    @pl.when(jnp.logical_not(matched))
    def _():
        own_copy.wait_recv()

    c_m = (table[0], table[1])
    ct_m = (table[2], table[3])
    moments = []
    coeffs = []
    for m in range(3):
        for way in (0, 1):
            fin_copy(way, 7 - way, m, core).wait_recv()
        total = own[m] + restore(fin.at[0, m]) + restore(fin.at[1, m])
        moment = 0.999 * mom[m] + total
        moments.append(moment)
        inner = mm3(c_m, split(moment), NN)
        coeff_t = mm3(c_m, split(inner), NT)
        coeffs.append(coeff_t)
        hi, lo = split(coeff_t)
        rows = mm(hi, pick_r[m], NN) + mm(lo, pick_r[m], NN)
        vals[m:m + 1, :] = jnp.sum(rows * pick_c[m].astype(F32), axis=0, keepdims=True)
    rep_copies = [
        pltpu.make_async_remote_copy(
            src_ref=vals, dst_ref=vals_all.at[r], send_sem=rep_send.at[i], recv_sem=rep_recv.at[r],
            device_id={"rep": (r + i) % 8}, device_id_type=MESH,
        )
        for i in range(1, 8)
    ]
    for c in rep_copies:
        c.start()
    vals_all[r] = vals[...]

    res = (rg_out, ru_out, rd_out)
    for m in range(3):
        mask = mm(pick_c[m], pick_r[m], NT)
        placed = jnp.where(mask > 0.5, coeffs[m], 0.0)
        half = mm3(ct_m, split(placed), NT)
        res[m][0, 0] = moments[m] - mm3(split(half), c_m, NN)

    for i in range(1, 8):
        q = (r + i) % 8
        pltpu.make_async_remote_copy(
            src_ref=vals, dst_ref=vals_all.at[q], send_sem=rep_send.at[i], recv_sem=rep_recv.at[q],
            device_id={"rep": q}, device_id_type=MESH,
        ).wait_recv()
    summed = vals_all[0]
    for i in range(1, 8):
        summed = summed + vals_all[i]
    for m, out in enumerate((ug_out, uu_out, ud_out)):
        hi, lo = split(summed[m:m + 1, :])
        cols = pick_c[m].astype(F32)
        placed = mm((cols * hi.astype(F32)).astype(BF16), pick_r[m], NT) + mm(
            (cols * lo.astype(F32)).astype(BF16), pick_r[m], NT
        )
        half = mm3(ct_m, split(placed), NT)
        out[0] = mm3(split(half), c_m, NN)

    for c in tok_copies + forwards + rep_copies:
        c.wait_send()

    @pl.when(matched)
    def _():
        own_copy.wait_send()

    def drain(s, carry):
        for way in (0, 1):
            steps = 8 - way
            active, kk, rb0 = ag_chunk(way, s)

            @pl.when(jnp.logical_and(active, s < steps))
            def _():
                for j in range(6):
                    ag_copy(way, s, kk, rb0, j).wait_send()
            sending, _, _ = rs_chunk(way, s)

            @pl.when(jnp.logical_and(sending, s < steps - 1))
            def _():
                for m in range(3):
                    rs_copy(way, s, m).wait_send()

            @pl.when(jnp.logical_and(sending, s == steps - 1))
            def _():
                for m in range(3):
                    for c in range(2):
                        fin_copy(way, s, m, c).wait_send()
        return carry

    lax.fori_loop(0, 8, drain, 0)


def per_device(x_in, d_out, gate_weight, up_weight, down_weight, mom_gate, mom_up, mom_down, band_index):
    dma = pltpu.SemaphoreType.DMA
    block = (SIDE, SIDE)
    scratch = [
        pltpu.VMEM((4, SIDE, 4 * SIDE), BF16),
        pltpu.VMEM((4, SIDE, 4 * SIDE), BF16),
        pltpu.VMEM((4, 4, 3) + block, BF16),
        pltpu.VMEM((4, 4, 3) + block, F32),
        pltpu.VMEM((2, 8, 3, 2, QROWS, SIDE), jnp.int16),
        pltpu.VMEM((2, 8, 3, 2, QROWS, SIDE), jnp.int16),
        pltpu.VMEM((2, 3, QROWS, SIDE), jnp.int16),
        pltpu.VMEM((3,) + block, F32),
        pltpu.VMEM((3,) + block, F32),
        pltpu.VMEM((3, 1, KEEP), jnp.int32),
        pltpu.VMEM((4,) + block, BF16),
        pltpu.VMEM((3, SIDE, KEEP), BF16),
        pltpu.VMEM((3, SIDE, KEEP), BF16),
        pltpu.VMEM((8, KEEP), F32),
        pltpu.VMEM((8, 8, KEEP), F32),
        dma((10,)),
        dma((3, 2)),
        dma((3, 2)),
        dma((2, 3)),
        dma((2, 8, 6)),
        dma((2, 8, 6)),
        dma((2, 8, 3, 2)),
        dma((2, 8, 3)),
        dma((2, 3)),
        dma((2,)),
        dma((8,)),
        dma((8,)),
    ]
    outs = [jax.ShapeDtypeStruct((1, 1) + block, F32)] * 3 + [jax.ShapeDtypeStruct((1,) + block, F32)] * 3
    return pl.pallas_call(
        kernel,
        out_shape=outs,
        in_specs=[pl.BlockSpec(memory_space=pl.ANY)] * 10,
        out_specs=[pl.BlockSpec(memory_space=pltpu.VMEM)] * 6,
        scratch_shapes=scratch,
        compiler_params=pltpu.CompilerParams(
            collective_id=0, has_side_effects=True, vmem_limit_bytes=48 * 1024 * 1024
        ),
        cost_estimate=pl.CostEstimate(flops=1700000000, bytes_accessed=2000000, transcendentals=300000),
    )(
        x_in, d_out, gate_weight, up_weight, down_weight, mom_gate, mom_up, mom_down, band_index,
        jnp.asarray(dct_parts()),
    )


def solution(mesh):
    tokens = P("rep", "fsdp", None)
    weights = P("fsdp", None, None)
    moments = P("rep", "fsdp", None, None)
    return jax.shard_map(
        per_device, mesh=mesh,
        in_specs=(tokens, tokens, weights, weights, weights, moments, moments, moments, P(None, "fsdp", None)),
        out_specs=(moments, moments, moments, weights, weights, weights),
        check_vma=False,
    )
```

time: 889 us -> 104 us (0.12); the launches traced: 880 us -> 104 us
  waiting for transfers between devices: 723 us -> 0 us
  Pallas kernels: 0 us -> 91.2 us
  local copies, waits for them, and re-layouts: 67.9 us -> 12 us
  starting transfers between devices: 28.2 us -> 0 us
  matrix products: 23.6 us -> 0 us
  blocking collectives: 22.1 us -> 0 us
  between operations: 14.1 us -> 0.66 us
    all_gather x3 -> x0, waiting for transfers between devices: 450 us -> none  [the longest x1 187 us: per_device(): lax.all_gather(gate_weight, 'fsdp', axis=0, tiled=True)]
    all_to_all x2 -> x0, waiting for transfers between devices: 271 us -> none  [the longest x1 271 us: per_device(): lax.all_to_all(act_send, 'fsdp', split_axis=1, concat_axis=0, tiled=True)]
    pallas_call x0 -> x1, Pallas kernels: none -> 91.2 us  [per_device(): pl.pallas_call(kernel, out_shape=outs, in_specs=[pl.BlockSpec(memory_spac...]
    all_to_all x2 -> x0, starting transfers between devices: 28.1 us -> none  [the longest x1 19.9 us: per_device(): lax.all_to_all(col_send, 'fsdp', split_axis=1, concat_axis=0, tiled=True)]
    dot_general x13 -> x0, matrix products: 23.6 us -> none  [the longest x1 7.43 us: per_device(): jnp.einsum('tic,ice->tie', x_sel, paired, preferred_element_type=jnp.floa...]
    all_gather x1 -> x0, blocking collectives: 22.1 us -> none  [per_device(): lax.all_gather(picked[None], 'rep', axis=0, tiled=True)]
    gather x5 -> x0, local copies, waits for them, and re-layouts: 16.5 us -> none  [the longest x3 13.5 us: band_split(): picked = jnp.take_along_axis(flattened, band_index, axis=2)]
    transpose x1 -> x0, local copies, waits for them, and re-layouts: 9.17 us -> none  [per_device(): jnp.einsum('tic,ice->tie', x_sel, paired, preferred_element_type=jnp.floa...]
  transfers between devices with their start and end apart: 5 -> 0, of which waited for: 4 -> 0; matrix products, arithmetic and copies ran while one was open for 5% -> 0% of each run, Pallas kernels for 0% -> 0%
where the time goes in v1:
time: 104 us
  Pallas kernels  91.2 us (88%)
  local copies, waits for them, and re-layouts  12 us (12%)
    pallas_call x1, Pallas kernels, per_device(): pl.pallas_call(kernel, out_shape=outs, in_specs=[pl.BlockSpec(memory_spac...  91.2 us
    unnamed x26, local copies, waits for them, and re-layouts  12 us

profile of v1, /device:TPU:1, one launch (start us, length us, event | category | flops | bytes accessed | tf_op | source)
XLA Modules:
  0.0 103.8 jit_solution(14337330103157904315)
XLA Ops:
  0.6 0.0 copy-start
  0.6 0.9 copy-done
  1.5 0.0 copy-start.1
  1.5 0.9 copy-done.1
  2.4 0.0 copy-start.2
  2.4 0.8 copy-done.2
  3.3 0.0 copy-start.3
  3.3 0.8 copy-done.3
  4.1 0.0 copy-start.4
  4.1 0.8 copy-done.4
  5.0 0.0 copy-start.5
  5.0 0.8 copy-done.5
  5.7 0.0 copy-start.6
  5.7 0.8 copy-done.6
  6.5 0.0 copy-start.7
  6.5 0.8 copy-done.7
  7.2 0.0 copy-start.8
  7.2 0.7 copy-done.8
  7.9 0.0 copy-start.9
  7.9 0.9 copy-done.9
  8.8 91.2 %shard_map.145 = (f32[1,1,128,128]{3,2,1,0:T(8,128)S(1)}, f32[1,1,128,128]{3,2,1,0:T(8,128)S(1)}, f32[1,1,128,128]{3,2,1,0:T(8,128)S(1)}, f32[1,128,128]{2,1,0:T...) custom-call(bf16[1,128,512]{2,1,0:T(8,128)(2,1)S(1)} %copy-done, bf16[1,128,512]{2,1,0:T(8,128)(2,1)S(1)} %copy-done.1, ...), custom_call_target="tpu_custom_call" | custom-call | flops 1700000000 | bytes 2000000 | tf_op jit(solution)/shard_map/pallas_call | solution.py:416
  100.0 0.6 copy.22
  100.6 0.6 copy.23
  101.3 0.6 copy.24
  101.9 0.6 copy.25
  102.5 0.6 copy.26
  103.2 0.6 copy.27
Async XLA Ops:
  0.6 0.9 copy-start
  1.5 0.9 copy-start.1
  2.4 0.8 copy-start.2
  3.3 0.8 copy-start.3
  4.1 0.8 copy-start.4
  5.0 0.8 copy-start.5
  5.7 0.8 copy-start.6
  6.5 0.8 copy-start.7
  7.2 0.7 copy-start.8
  7.9 0.9 copy-start.9

commit v2 on v1

v2 whole, which is shorter than its diff:
```python
import jax
import jax.numpy as jnp
import numpy as np
from jax import lax
from jax.experimental import pallas as pl
from jax.experimental.pallas import tpu as pltpu
from jax.sharding import PartitionSpec as P

MESH = pl.DeviceIdType.MESH
F32 = jnp.float32
BF16 = jnp.bfloat16
SIDE = 128
WIDE = 512
KEEP = 512
NZ = 16
HALF = SIDE // 2
PIECES = 12


def dct_parts():
    k = np.arange(SIDE, dtype=np.float64)[:, None]
    n = np.arange(SIDE, dtype=np.float64)[None, :]
    s = np.where(k == 0, np.sqrt(1.0 / SIDE), np.sqrt(2.0 / SIDE))
    c = (s * np.cos(np.pi * (2.0 * n + 1.0) * k / (2.0 * SIDE))).astype(np.float32)
    out = []
    for t in (c, c.T):
        hi = t.astype(jnp.bfloat16)
        lo = (t - hi.astype(np.float32)).astype(jnp.bfloat16)
        out += [hi, lo]
    return np.stack(out)


def mm(a, b, dims):
    return lax.dot_general(a, b, (dims, ((), ())), preferred_element_type=F32)


NN = ((1,), (0,))
NT = ((1,), (1,))
TN = ((0,), (0,))


def split(a):
    hi = a.astype(BF16)
    return hi, (a - hi.astype(F32)).astype(BF16)


def mm3(a, b, dims):
    return mm(a[0], b[0], dims) + (mm(a[0], b[1], dims) + mm(a[1], b[0], dims))


def kernel(
    x_ref, d_ref, wg_ref, wu_ref, wd_ref, mg_ref, mu_ref, md_ref, band_ref, table_ref,
    out,
    tok, mine_w, wts, part, recv, send, fin, mom, band, table, pick_r, pick_c, mask, vals, vals_all,
    load_sem, tok_send, tok_recv, w1_send, w1_recv, w2_send, w2_recv, rs_send, rs_recv, fin_recv,
    rep_send, rep_recv,
):
    f = lax.axis_index("fsdp")
    r = lax.axis_index("rep")
    core = f % 2
    z = (f // 2) % NZ
    xh = f // (2 * NZ)
    base = xh * (2 * NZ)
    sib = f + 1 - 2 * core
    partner = f + (1 - 2 * xh) * (2 * NZ)
    m_own = z // 2
    p_own = z % 2

    def chip(zz, c):
        return base + ((zz + NZ) % NZ) * 2 + c

    def remote(src, dst, ssem, rsem, target):
        return pltpu.make_async_remote_copy(
            src_ref=src, dst_ref=dst, send_sem=ssem, recv_sem=rsem,
            device_id={"fsdp": target}, device_id_type=MESH,
        )

    def to_rep(src, dst, ssem, rsem, target):
        return pltpu.make_async_remote_copy(
            src_ref=src, dst_ref=dst, send_sem=ssem, recv_sem=rsem,
            device_id={"rep": target}, device_id_type=MESH,
        )

    recv[...] = jnp.zeros(recv.shape, BF16)
    barrier = pltpu.get_barrier_semaphore()

    def greet(i, carry):
        pl.semaphore_signal(
            barrier, inc=1, device_id={"fsdp": base + (f - base + i) % (2 * NZ)}, device_id_type=MESH
        )
        return carry

    lax.fori_loop(1, 2 * NZ, greet, 0)
    pl.semaphore_signal(barrier, inc=1, device_id={"fsdp": partner}, device_id_type=MESH)
    for i in range(1, 8):
        pl.semaphore_signal(barrier, inc=1, device_id={"rep": (r + i) % 8}, device_id_type=MESH)

    slot = pl.multiple_of((2 * xh + core) * 2 * SIDE, 2 * SIDE)
    other = pl.multiple_of((2 * (1 - xh) + core) * 2 * SIDE, 2 * SIDE)
    loads = [
        pltpu.make_async_copy(band_ref, band, load_sem.at[0]),
        pltpu.make_async_copy(wg_ref.at[0], mine_w.at[0], load_sem.at[1]),
        pltpu.make_async_copy(wu_ref.at[0], mine_w.at[1], load_sem.at[2]),
        pltpu.make_async_copy(wd_ref.at[0], mine_w.at[2], load_sem.at[3]),
        pltpu.make_async_copy(x_ref.at[0], tok.at[0, pl.ds(slot, SIDE)], load_sem.at[4]),
        pltpu.make_async_copy(d_ref.at[0], tok.at[1, pl.ds(slot, SIDE)], load_sem.at[5]),
        pltpu.make_async_copy(mg_ref.at[0, 0], mom.at[0], load_sem.at[6]),
        pltpu.make_async_copy(mu_ref.at[0, 0], mom.at[1], load_sem.at[7]),
        pltpu.make_async_copy(md_ref.at[0, 0], mom.at[2], load_sem.at[8]),
        pltpu.make_async_copy(table_ref, table, load_sem.at[9]),
    ]
    for c in loads:
        c.start()

    vals[...] = jnp.zeros(vals.shape, F32)
    loads[0].wait()
    spots = lax.broadcasted_iota(jnp.int32, (SIDE, KEEP), 0)
    for m in range(3):
        at = band[m]
        pick_r[m] = jnp.where(spots == lax.shift_right_logical(at, 7), 1.0, 0.0).astype(BF16)
        pick_c[m] = jnp.where(spots == lax.bitwise_and(at, 127), 1.0, 0.0).astype(BF16)
    for m in range(3):
        mask[m] = mm(pick_c[m], pick_r[m], NT)
    for c in loads[1:]:
        c.wait()

    k_own = z // 2
    h_own = k_own % 2
    kk_own = (k_own % 4) // 2
    rb_own = f % 4
    eighth = pl.ds(pl.multiple_of(r * 16, 16), 16)
    skew = jnp.where(p_own == k_own // 4, 0, 1)

    def w1_copy(i, target):
        return remote(
            mine_w.at[:, eighth], wts.at[kk_own, rb_own, :, eighth], w1_send.at[i], w1_recv.at[kk_own, rb_own], target
        )

    hops = (8, -6, 6, -4, 4, -2, 2, 0)
    w1_to = [chip(z + hop + skew, h_own) for hop in hops]
    w1_self = w1_to[-1] == f

    @pl.when(w1_self)
    def _():
        wts[kk_own, rb_own, :, eighth, :] = mine_w[:, eighth, :]

    pl.semaphore_wait(barrier, 2 * NZ + 7)

    for i, target in enumerate(w1_to[:-1]):
        w1_copy(i, target).start()

    @pl.when(jnp.logical_not(w1_self))
    def _():
        w1_copy(7, w1_to[-1]).start()

    def rows(start, size):
        return tok.at[:, pl.ds(start, size)]

    def tok_copy(i, src, dst, size, target):
        return remote(rows(src, size), rows(dst, size), tok_send.at[i], tok_recv.at[i], target)

    up = chip(z + 1, core)
    down = chip(z - 1, core)
    to_partner = tok_copy(0, slot, slot, SIDE, partner)
    to_up = tok_copy(1, slot, slot + SIDE, HALF, up)
    to_down = tok_copy(2, slot + HALF, slot + SIDE + HALF, HALF, down)
    to_sib = tok_copy(3, slot, slot, SIDE, sib)
    for c in (to_partner, to_up, to_down, to_sib):
        c.start()
    from_partner = tok_copy(0, slot, other, SIDE, partner)
    on_up = tok_copy(4, other, other + SIDE, HALF, up)
    on_down = tok_copy(5, other + HALF, other + SIDE + HALF, HALF, down)
    on_sib = tok_copy(6, other, other, SIDE, sib)
    near_sib = tok_copy(7, slot + SIDE, slot + SIDE, SIDE, sib)
    far_sib = tok_copy(8, other + SIDE, other + SIDE, SIDE, sib)

    def column_of(kk):
        k = 4 * p_own + core + 2 * kk
        ahead = (k - m_own + 8) % 8
        return k, ahead, jnp.where(ahead > 4, ahead - 4, 4 - ahead)

    stage_0 = column_of(0)[2]
    stage_1 = column_of(1)[2]
    first = jnp.where(stage_0 <= stage_1, 0, 1)
    stage_first = jnp.minimum(stage_0, stage_1)
    together = stage_0 == stage_1

    def w2_copy(kk, i):
        piece = wts.at[kk, :, :, eighth]
        return to_rep(piece, piece, w2_send.at[kk, i], w2_recv.at[kk, r], (r + i) % 8)

    def w1_arrived(kk):
        k = column_of(kk)[0]
        for rb in range(4):
            @pl.when(base + 4 * k + rb != f)
            def _():
                remote(
                    mine_w.at[:, eighth], wts.at[kk, rb, :, eighth], w1_send.at[0], w1_recv.at[kk, rb], sib
                ).wait_recv()
        for i in range(1, 8):
            w2_copy(kk, i).start()

    w1_arrived(1 - first)
    from_partner.wait_recv()
    for c in (on_up, on_down, on_sib):
        c.start()
    w1_arrived(first)
    to_up.wait_recv()
    to_down.wait_recv()
    near_sib.start()
    on_up.wait_recv()
    on_down.wait_recv()
    far_sib.start()
    for c in (to_sib, on_sib, near_sib, far_sib):
        c.wait_recv()

    def column(kk):
        xs = tok[0]
        ds = tok[1]
        w_gu = jnp.concatenate(
            [wts[kk, :, 0].reshape(WIDE, SIDE), wts[kk, :, 1].reshape(WIDE, SIDE)], axis=1
        )
        w_d = jnp.concatenate([wts[kk, i, 2] for i in range(4)], axis=1)
        gu = mm(xs, w_gu, NN)
        dh = mm(ds, w_d, NT)
        gate = gu[:, :SIDE]
        upp = gu[:, SIDE:]
        sg = jax.nn.sigmoid(gate)
        act = gate * sg
        hidden = (act * upp).astype(BF16)
        d_gate = (dh * upp * sg * (1.0 + gate * (1.0 - sg))).astype(BF16)
        d_up = (dh * act).astype(BF16)
        g_in = mm(xs, jnp.concatenate([d_gate, d_up], axis=1), TN)
        g_out = mm(hidden, ds, TN)
        for i in range(4):
            part[kk, i, 0] = g_in[i * SIDE:(i + 1) * SIDE, :SIDE]
            part[kk, i, 1] = g_in[i * SIDE:(i + 1) * SIDE, SIDE:]
            part[kk, i, 2] = g_out[:, i * SIDE:(i + 1) * SIDE]

    def on_copy(kk, rb, m, target):
        return remote(send.at[kk, rb, m], recv.at[kk, rb, m], rs_send.at[kk, rb, m], rs_recv.at[kk, rb, m], target)

    def fin_copy(kk, rb, m, way, target):
        return remote(send.at[kk, rb, m], fin.at[way, m], rs_send.at[kk, rb, m], fin_recv.at[way, m], target)

    def pass_on(kk, j):
        m = j // 4
        rb = j % 4
        k, ahead, stage = column_of(kk)
        low = rb < 2
        heard = (
            (ahead == 1) | (ahead == 2) | (ahead == 6) | (ahead == 7)
            | ((ahead == 3) & low) | ((ahead == 5) & jnp.logical_not(low))
        )
        upward = (ahead < 4) | ((ahead == 4) & low)
        last = (ahead == 0) | (ahead == 1) | (ahead == 7)
        owner = base + 4 * k + rb

        @pl.when(heard)
        def _():
            on_copy(kk, rb, m, sib).wait_recv()
        value = (part[kk, rb, m] + recv[kk, rb, m].astype(F32)).astype(BF16)
        send[kk, rb, m] = value

        @pl.when(jnp.logical_not(last))
        def _():
            on_copy(kk, rb, m, jnp.where(upward, chip(z + 2, core), chip(z - 2, core))).start()

        @pl.when(last & (owner != f))
        def _():
            way = jnp.where(ahead == 0, 2, jnp.where(ahead == 1, 0, 1))
            fin_copy(kk, rb, m, way, owner).start()

        @pl.when(last & (owner == f))
        def _():
            fin[2, m] = value

    def pass_all(j, carry):
        pass_on(first, j)
        return carry

    def work(i, carry):
        kk = jnp.where(i == 0, first, 1 - first)
        for q in range(1, 8):
            w2_in = wts.at[kk, :, :, eighth]
            to_rep(w2_in, w2_in, w2_send.at[kk, q], w2_recv.at[kk, (r + q) % 8], r).wait_recv()
        column(kk)

        @pl.when((i == 0) & (stage_first == 0))
        def _():
            lax.fori_loop(0, PIECES, pass_all, 0)
        return carry

    lax.fori_loop(0, 2, work, 0)

    def pass_rest(t, carry):
        second = jnp.where(together, t % 2, t // PIECES)
        j = jnp.where(together, t // 2, t % PIECES)
        pass_on(jnp.where(second == 0, first, 1 - first), j)
        return carry

    lax.fori_loop(jnp.where(stage_first == 0, PIECES, 0), 2 * PIECES, pass_rest, 0)

    c_m = (table[0], table[1])
    ct_m = (table[2], table[3])
    is_middle = (m_own == k_own) & (p_own == k_own // 4) & (core == h_own)
    moments = []
    coeffs = []
    for m in range(3):
        for way in (0, 1):
            fin_copy(0, 0, m, way, sib).wait_recv()

        @pl.when(jnp.logical_not(is_middle))
        def _():
            fin_copy(0, 0, m, 2, sib).wait_recv()
        total = fin[0, m].astype(F32) + fin[1, m].astype(F32) + fin[2, m].astype(F32)
        moment = 0.999 * mom[m] + total
        moments.append(moment)
        inner = mm3(c_m, split(moment), NN)
        coeff_t = mm3(c_m, split(inner), NT)
        coeffs.append(coeff_t)
        hi, lo = split(coeff_t)
        picked = mm(hi, pick_r[m], NN) + mm(lo, pick_r[m], NN)
        vals[m:m + 1, :] = jnp.sum(picked * pick_c[m].astype(F32), axis=0, keepdims=True)
    rep_copies = [to_rep(vals, vals_all.at[r], rep_send.at[i], rep_recv.at[r], (r + i) % 8) for i in range(1, 8)]
    for c in rep_copies:
        c.start()
    vals_all[r] = vals[...]

    for m in range(3):
        placed = jnp.where(mask[m] > 0.5, coeffs[m], 0.0)
        half = mm3(ct_m, split(placed), NT)
        out[m] = moments[m] - mm3(split(half), c_m, NN)

    for i in range(1, 8):
        q = (r + i) % 8
        to_rep(vals, vals_all.at[q], rep_send.at[i], rep_recv.at[q], q).wait_recv()
    summed = vals_all[0]
    for i in range(1, 8):
        summed = summed + vals_all[i]
    for m in range(3):
        hi, lo = split(summed[m:m + 1, :])
        cols = pick_c[m].astype(F32)
        placed = mm((cols * hi.astype(F32)).astype(BF16), pick_r[m], NT) + mm(
            (cols * lo.astype(F32)).astype(BF16), pick_r[m], NT
        )
        half = mm3(ct_m, split(placed), NT)
        out[3 + m] = mm3(split(half), c_m, NN)

    for c in (to_partner, to_up, to_down, to_sib, on_up, on_down, on_sib, near_sib, far_sib):
        c.wait_send()
    for c in rep_copies:
        c.wait_send()
    for i, target in enumerate(w1_to[:-1]):
        w1_copy(i, target).wait_send()

    @pl.when(jnp.logical_not(w1_self))
    def _():
        w1_copy(7, w1_to[-1]).wait_send()

    def drain(kk, carry):
        k = column_of(kk)[0]
        for i in range(1, 8):
            w2_copy(kk, i).wait_send()
        for j in range(PIECES):
            @pl.when(base + 4 * k + j % 4 != f)
            def _():
                on_copy(kk, j % 4, j // 4, sib).wait_send()
        return carry

    lax.fori_loop(0, 2, drain, 0)


def write_out(all_ref, *refs):
    outs, sems = refs[:6], refs[6]
    copies = [
        pltpu.make_async_copy(all_ref.at[i], o.at[(0, 0) if i < 3 else (0,)], sems.at[i]) for i, o in enumerate(outs)
    ]
    for c in copies:
        c.start()
    for c in copies:
        c.wait()


def per_device(x_in, d_out, gate_weight, up_weight, down_weight, mom_gate, mom_up, mom_down, band_index):
    dma = pltpu.SemaphoreType.DMA
    block = (SIDE, SIDE)
    scratch = [
        pltpu.VMEM((2, 8 * SIDE, WIDE), BF16),
        pltpu.VMEM((3,) + block, BF16),
        pltpu.VMEM((2, 4, 3) + block, BF16),
        pltpu.VMEM((2, 4, 3) + block, F32),
        pltpu.VMEM((2, 4, 3) + block, BF16),
        pltpu.VMEM((2, 4, 3) + block, BF16),
        pltpu.VMEM((3, 3) + block, BF16),
        pltpu.VMEM((3,) + block, F32),
        pltpu.VMEM((3, 1, KEEP), jnp.int32),
        pltpu.VMEM((4,) + block, BF16),
        pltpu.VMEM((3, SIDE, KEEP), BF16),
        pltpu.VMEM((3, SIDE, KEEP), BF16),
        pltpu.VMEM((3,) + block, F32),
        pltpu.VMEM((8, KEEP), F32),
        pltpu.VMEM((8, 8, KEEP), F32),
        dma((10,)),
        dma((9,)),
        dma((9,)),
        dma((8,)),
        dma((2, 4)),
        dma((2, 8)),
        dma((2, 8)),
        dma((2, 4, 3)),
        dma((2, 4, 3)),
        dma((3, 3)),
        dma((8,)),
        dma((8,)),
    ]
    hbm = pl.BlockSpec(memory_space=pltpu.HBM)
    vmem = pl.BlockSpec(memory_space=pltpu.VMEM)
    results = pl.pallas_call(
        kernel,
        out_shape=jax.ShapeDtypeStruct((6,) + block, F32),
        in_specs=[hbm] * 10,
        out_specs=vmem,
        scratch_shapes=scratch,
        compiler_params=pltpu.CompilerParams(
            collective_id=0, has_side_effects=True, vmem_limit_bytes=62 * 1024 * 1024
        ),
        cost_estimate=pl.CostEstimate(flops=1700000000, bytes_accessed=2000000, transcendentals=300000),
    )(
        x_in, d_out, gate_weight, up_weight, down_weight, mom_gate, mom_up, mom_down, band_index,
        jnp.asarray(dct_parts()),
    )
    outs = [jax.ShapeDtypeStruct((1, 1) + block, F32)] * 3 + [jax.ShapeDtypeStruct((1,) + block, F32)] * 3
    return pl.pallas_call(
        write_out, out_shape=outs, in_specs=[vmem], out_specs=[hbm] * 6, scratch_shapes=[dma((6,))]
    )(results)


def solution(mesh):
    tokens = P("rep", "fsdp", None)
    weights = P("fsdp", None, None)
    moments = P("rep", "fsdp", None, None)
    return jax.shard_map(
        per_device, mesh=mesh,
        in_specs=(tokens, tokens, weights, weights, weights, moments, moments, moments, P(None, "fsdp", None)),
        out_specs=(moments, moments, moments, weights, weights, weights),
        check_vma=False,
    )
```

time: 104 us -> 74.6 us (0.72)
  Pallas kernels: 91.2 us -> 73.5 us
  local copies, waits for them, and re-layouts: 12 us -> 0 us
    pallas_call x1 -> x2, Pallas kernels: 91.2 us -> 73.5 us  [the longest x1 71.8 us: per_device(): pl.pallas_call(kernel, out_shape=jax.ShapeDtypeStruct((6,) + block, F32),...]
    unnamed x26 -> x0, local copies, waits for them, and re-layouts: 12 us -> none
where the time goes in v2:
time: 74.6 us; the launch traced here: 74.2 us
  Pallas kernels  73.5 us (99%)
    pallas_call x1, Pallas kernels, per_device(): pl.pallas_call(kernel, out_shape=jax.ShapeDtypeStruct((6,) + block, F32),...  71.8 us
    pallas_call x1, Pallas kernels, per_device(): pl.pallas_call(write_out, out_shape=outs, in_specs=[vmem], out_specs=[hbm...  1.78 us

profile of v2, /device:TPU:1, one launch (start us, length us, event | category | flops | bytes accessed | tf_op | source)
XLA Modules:
  0.0 74.2 jit_solution(3608179955438988918)
XLA Ops:
  0.6 71.8 %shard_map.145.all_ref = f32[6,128,128]{2,1,0:T(8,128)} custom-call(bf16[1,128,512]{2,1,0:T(8,128)(2,1)} %x_ref.1, bf16[1,128,512]{2,1,0:T(8,128)(2,1)} %d_ref.1, bf16[1,128,128]{2,1,0:T(8,128)(2,1)} %wg_ref.1, bf16[1,128,128]{2,1,0:T(8,128)(2,1)} %wu_ref.1, bf16[1,128,128]{2,1,0:T(8,128)(2,1)} %wd_ref.1, f32[1,1,128,128]{3,2,1,0:T(8,128)} %mg_ref.1, ...), custom_call_target="tpu_custom_call" | custom-call | flops 1700000000 | bytes 2000000 | tf_op jit(solution)/shard_map/pallas_call | solution.py:419
  72.4 1.8 %shard_map.146 = (f32[1,1,128,128]{3,2,1,0:T(8,128)}, f32[1,1,128,128]{3,2,1,0:T(8,128)}, f32[1,1,128,128]{3,2,1,0:T(8,128)}, f32[1,128,128]{2,1,0:T(8,128)}, f3...) custom-call(f32[6,128,128]{2,1,0:T(8,128)} %shard_map.145.all_ref), custom_call_target="tpu_custom_call" | custom-call | tf_op jit(solution)/shard_map/pallas_call | solution.py:434

commit v3 on v2

--- a/solution.py
+++ b/solution.py
@@ -81,19 +81,32 @@
             device_id={"rep": target}, device_id_type=MESH,
         )
 
+    k_own = z // 2
+    h_own = (k_own // 2) % 2
+    kk_own = k_own // 4
+    rb_own = f % 4
+    skew = jnp.where(p_own == k_own % 2, 0, 1)
+    w1_to = [chip(z + hop + skew, h_own) for hop in (8, -6, 6, -4, 4, -2, 2, 0)]
+    w1_self = w1_to[-1] == f
+
     recv[...] = jnp.zeros(recv.shape, BF16)
     barrier = pltpu.get_barrier_semaphore()
 
-    def greet(i, carry):
-        pl.semaphore_signal(
-            barrier, inc=1, device_id={"fsdp": base + (f - base + i) % (2 * NZ)}, device_id_type=MESH
-        )
-        return carry
-
-    lax.fori_loop(1, 2 * NZ, greet, 0)
-    pl.semaphore_signal(barrier, inc=1, device_id={"fsdp": partner}, device_id_type=MESH)
+    def greet(**to):
+        pl.semaphore_signal(barrier, inc=1, device_id=to, device_id_type=MESH)
+
+    sources = [base + 4 * (p_own + 2 * core + 4 * kk) + rb for kk in (0, 1) for rb in range(4)]
+    for target in w1_to[:-1]:
+        greet(fsdp=target)
+    for source in sources + [w1_to[-1]]:
+        @pl.when(source != f)
+        def _():
+            greet(fsdp=source)
+    near = [chip(z + 2, core), chip(z - 2, core), chip(z + 1, core), chip(z - 1, core), partner, sib]
+    for target in near:
+        greet(fsdp=target)
     for i in range(1, 8):
-        pl.semaphore_signal(barrier, inc=1, device_id={"rep": (r + i) % 8}, device_id_type=MESH)
+        greet(rep=(r + i) % 8)
 
     slot = pl.multiple_of((2 * xh + core) * 2 * SIDE, 2 * SIDE)
     other = pl.multiple_of((2 * (1 - xh) + core) * 2 * SIDE, 2 * SIDE)
@@ -124,27 +137,18 @@
     for c in loads[1:]:
         c.wait()
 
-    k_own = z // 2
-    h_own = k_own % 2
-    kk_own = (k_own % 4) // 2
-    rb_own = f % 4
     eighth = pl.ds(pl.multiple_of(r * 16, 16), 16)
-    skew = jnp.where(p_own == k_own // 4, 0, 1)
 
     def w1_copy(i, target):
         return remote(
-            mine_w.at[:, eighth], wts.at[kk_own, rb_own, :, eighth], w1_send.at[i], w1_recv.at[kk_own, rb_own], target
+            mine_w.at[:, eighth], wts.at[kk_own, r, rb_own], w1_send.at[i], w1_recv.at[kk_own, rb_own], target
         )
-
-    hops = (8, -6, 6, -4, 4, -2, 2, 0)
-    w1_to = [chip(z + hop + skew, h_own) for hop in hops]
-    w1_self = w1_to[-1] == f
 
     @pl.when(w1_self)
     def _():
-        wts[kk_own, rb_own, :, eighth, :] = mine_w[:, eighth, :]
-
-    pl.semaphore_wait(barrier, 2 * NZ + 7)
+        wts[kk_own, r, rb_own] = mine_w[:, eighth, :]
+
+    pl.semaphore_wait(barrier, jnp.where(w1_self, 27, 29))
 
     for i, target in enumerate(w1_to[:-1]):
         w1_copy(i, target).start()
@@ -161,32 +165,31 @@
 
     up = chip(z + 1, core)
     down = chip(z - 1, core)
-    to_partner = tok_copy(0, slot, slot, SIDE, partner)
-    to_up = tok_copy(1, slot, slot + SIDE, HALF, up)
-    to_down = tok_copy(2, slot + HALF, slot + SIDE + HALF, HALF, down)
-    to_sib = tok_copy(3, slot, slot, SIDE, sib)
-    for c in (to_partner, to_up, to_down, to_sib):
+    quarter = HALF // 2
+    parts = [(0, up, SIDE), (HALF, down, SIDE), (quarter, up, SIDE), (HALF + quarter, down, SIDE)]
+    to_partner = [tok_copy(i, slot + at, slot + at, quarter, partner) for i, (at, _, _) in enumerate(parts)]
+    from_partner = [tok_copy(i, slot + at, other + at, quarter, partner) for i, (at, _, _) in enumerate(parts)]
+    pass_near = [tok_copy(4 + i, other + at, other + at + off, quarter, to) for i, (at, to, off) in enumerate(parts)]
+    pass_far = [tok_copy(8 + i, other + at + off, other + at + off, quarter, sib) for i, (at, _, off) in enumerate(parts)]
+    to_up = tok_copy(12, slot, slot + SIDE, HALF, up)
+    to_down = tok_copy(13, slot + HALF, slot + SIDE + HALF, HALF, down)
+    to_sib = tok_copy(14, slot, slot, SIDE, sib)
+    on_sib = tok_copy(15, other, other, SIDE, sib)
+    near_sib = tok_copy(16, slot + SIDE, slot + SIDE, SIDE, sib)
+    for c in to_partner + [to_up, to_down, to_sib]:
         c.start()
-    from_partner = tok_copy(0, slot, other, SIDE, partner)
-    on_up = tok_copy(4, other, other + SIDE, HALF, up)
-    on_down = tok_copy(5, other + HALF, other + SIDE + HALF, HALF, down)
-    on_sib = tok_copy(6, other, other, SIDE, sib)
-    near_sib = tok_copy(7, slot + SIDE, slot + SIDE, SIDE, sib)
-    far_sib = tok_copy(8, other + SIDE, other + SIDE, SIDE, sib)
 
     def column_of(kk):
-        k = 4 * p_own + core + 2 * kk
+        k = p_own + 2 * core + 4 * kk
         ahead = (k - m_own + 8) % 8
         return k, ahead, jnp.where(ahead > 4, ahead - 4, 4 - ahead)
 
     stage_0 = column_of(0)[2]
     stage_1 = column_of(1)[2]
     first = jnp.where(stage_0 <= stage_1, 0, 1)
-    stage_first = jnp.minimum(stage_0, stage_1)
-    together = stage_0 == stage_1
 
     def w2_copy(kk, i):
-        piece = wts.at[kk, :, :, eighth]
+        piece = wts.at[kk, r]
         return to_rep(piece, piece, w2_send.at[kk, i], w2_recv.at[kk, r], (r + i) % 8)
 
     def w1_arrived(kk):
@@ -195,32 +198,36 @@
             @pl.when(base + 4 * k + rb != f)
             def _():
                 remote(
-                    mine_w.at[:, eighth], wts.at[kk, rb, :, eighth], w1_send.at[0], w1_recv.at[kk, rb], sib
+                    mine_w.at[:, eighth], wts.at[kk, r, rb], w1_send.at[0], w1_recv.at[kk, rb], sib
                 ).wait_recv()
         for i in range(1, 8):
             w2_copy(kk, i).start()
 
-    w1_arrived(1 - first)
-    from_partner.wait_recv()
-    for c in (on_up, on_down, on_sib):
-        c.start()
+    def tokens_in(i):
+        from_partner[i].wait_recv()
+        pass_near[i].start()
+
+    for i in range(3):
+        tokens_in(i)
     w1_arrived(first)
+    tokens_in(3)
+    on_sib.start()
     to_up.wait_recv()
     to_down.wait_recv()
     near_sib.start()
-    on_up.wait_recv()
-    on_down.wait_recv()
-    far_sib.start()
-    for c in (to_sib, on_sib, near_sib, far_sib):
+    w1_arrived(1 - first)
+    for c, d in zip(pass_near, pass_far):
+        c.wait_recv()
+        d.start()
+    for c in [to_sib, on_sib, near_sib] + pass_far:
         c.wait_recv()
 
     def column(kk):
         xs = tok[0]
         ds = tok[1]
-        w_gu = jnp.concatenate(
-            [wts[kk, :, 0].reshape(WIDE, SIDE), wts[kk, :, 1].reshape(WIDE, SIDE)], axis=1
-        )
-        w_d = jnp.concatenate([wts[kk, i, 2] for i in range(4)], axis=1)
+        w_g, w_u, w_d = ([wts[kk, :, i, m].reshape(SIDE, SIDE) for i in range(4)] for m in range(3))
+        w_gu = jnp.concatenate([jnp.concatenate(w_g, axis=0), jnp.concatenate(w_u, axis=0)], axis=1)
+        w_d = jnp.concatenate(w_d, axis=1)
         gu = mm(xs, w_gu, NN)
         dh = mm(ds, w_d, NT)
         gate = gu[:, :SIDE]
@@ -243,16 +250,17 @@
     def fin_copy(kk, rb, m, way, target):
         return remote(send.at[kk, rb, m], fin.at[way, m], rs_send.at[kk, rb, m], fin_recv.at[way, m], target)
 
-    def pass_on(kk, j):
-        m = j // 4
-        rb = j % 4
+    def turn_of(ahead, half):
+        up_turn = 4 - half - ahead
+        down_turn = ahead - 5 + half
+        return jnp.where(ahead == 0, 4, jnp.where(ahead < 4, up_turn, jnp.where(ahead == 4, 0, down_turn)))
+
+    def pass_on(kk, half, j):
+        m = j // 2
+        rb = 2 * half + j % 2
         k, ahead, stage = column_of(kk)
-        low = rb < 2
-        heard = (
-            (ahead == 1) | (ahead == 2) | (ahead == 6) | (ahead == 7)
-            | ((ahead == 3) & low) | ((ahead == 5) & jnp.logical_not(low))
-        )
-        upward = (ahead < 4) | ((ahead == 4) & low)
+        heard = (turn_of(ahead, half) > 0) & (ahead != 0)
+        upward = (ahead < 4) | ((ahead == 4) & (half == 0))
         last = (ahead == 0) | (ahead == 1) | (ahead == 7)
         owner = base + 4 * k + rb
 
@@ -275,35 +283,40 @@
         def _():
             fin[2, m] = value
 
-    def pass_all(j, carry):
-        pass_on(first, j)
-        return carry
+    def pass_turn(kks, turn):
+        halves = [(kk, half) for kk in kks for half in (0, 1)]
+        due = [turn_of(column_of(kk)[1], half) == turn for kk, half in halves]
+
+        def step(j, carry):
+            for (kk, half), now in zip(halves, due):
+                @pl.when(now)
+                def _():
+                    pass_on(kk, half, j)
+            return carry
+
+        lax.fori_loop(0, PIECES // 2, step, 0)
 
     def work(i, carry):
         kk = jnp.where(i == 0, first, 1 - first)
         for q in range(1, 8):
-            w2_in = wts.at[kk, :, :, eighth]
+            w2_in = wts.at[kk, (r + q) % 8]
             to_rep(w2_in, w2_in, w2_send.at[kk, q], w2_recv.at[kk, (r + q) % 8], r).wait_recv()
         column(kk)
 
-        @pl.when((i == 0) & (stage_first == 0))
-        def _():
-            lax.fori_loop(0, PIECES, pass_all, 0)
+        pass_turn((kk,), 0)
         return carry
 
     lax.fori_loop(0, 2, work, 0)
 
-    def pass_rest(t, carry):
-        second = jnp.where(together, t % 2, t // PIECES)
-        j = jnp.where(together, t // 2, t % PIECES)
-        pass_on(jnp.where(second == 0, first, 1 - first), j)
+    def pass_rest(turn, carry):
+        pass_turn((first, 1 - first), turn)
         return carry
 
-    lax.fori_loop(jnp.where(stage_first == 0, PIECES, 0), 2 * PIECES, pass_rest, 0)
+    lax.fori_loop(1, 5, pass_rest, 0)
 
     c_m = (table[0], table[1])
     ct_m = (table[2], table[3])
-    is_middle = (m_own == k_own) & (p_own == k_own // 4) & (core == h_own)
+    is_middle = (m_own == k_own) & (p_own == k_own % 2) & (core == h_own)
     moments = []
     coeffs = []
     for m in range(3):
@@ -321,7 +334,9 @@
         coeffs.append(coeff_t)
         hi, lo = split(coeff_t)
         picked = mm(hi, pick_r[m], NN) + mm(lo, pick_r[m], NN)
-        vals[m:m + 1, :] = jnp.sum(picked * pick_c[m].astype(F32), axis=0, keepdims=True)
+        band_row = jnp.sum(picked * pick_c[m].astype(F32), axis=0, keepdims=True)
+        for q in range(4):
+            vals[4 * m + q:4 * m + q + 1, :] = band_row[:, q * SIDE:(q + 1) * SIDE]
     rep_copies = [to_rep(vals, vals_all.at[r], rep_send.at[i], rep_recv.at[r], (r + i) % 8) for i in range(1, 8)]
     for c in rep_copies:
         c.start()
@@ -339,7 +354,7 @@
     for i in range(1, 8):
         summed = summed + vals_all[i]
     for m in range(3):
-        hi, lo = split(summed[m:m + 1, :])
+        hi, lo = split(jnp.concatenate([summed[4 * m + q:4 * m + q + 1, :] for q in range(4)], axis=1))
         cols = pick_c[m].astype(F32)
         placed = mm((cols * hi.astype(F32)).astype(BF16), pick_r[m], NT) + mm(
             (cols * lo.astype(F32)).astype(BF16), pick_r[m], NT
@@ -347,7 +362,7 @@
         half = mm3(ct_m, split(placed), NT)
         out[3 + m] = mm3(split(half), c_m, NN)
 
-    for c in (to_partner, to_up, to_down, to_sib, on_up, on_down, on_sib, near_sib, far_sib):
+    for c in to_partner + pass_near + pass_far + [to_up, to_down, to_sib, on_sib, near_sib]:
         c.wait_send()
     for c in rep_copies:
         c.wait_send()
@@ -388,7 +403,7 @@
     scratch = [
         pltpu.VMEM((2, 8 * SIDE, WIDE), BF16),
         pltpu.VMEM((3,) + block, BF16),
-        pltpu.VMEM((2, 4, 3) + block, BF16),
+        pltpu.VMEM((2, 8, 4, 3, 16, SIDE), BF16),
         pltpu.VMEM((2, 4, 3) + block, F32),
         pltpu.VMEM((2, 4, 3) + block, BF16),
         pltpu.VMEM((2, 4, 3) + block, BF16),
@@ -399,11 +414,11 @@
         pltpu.VMEM((3, SIDE, KEEP), BF16),
         pltpu.VMEM((3, SIDE, KEEP), BF16),
         pltpu.VMEM((3,) + block, F32),
-        pltpu.VMEM((8, KEEP), F32),
-        pltpu.VMEM((8, 8, KEEP), F32),
+        pltpu.VMEM((16, SIDE), F32),
+        pltpu.VMEM((8, 16, SIDE), F32),
         dma((10,)),
-        dma((9,)),
-        dma((9,)),
+        dma((17,)),
+        dma((17,)),
         dma((8,)),
         dma((2, 4)),
         dma((2, 8)),

time: 74.6 us -> 69.4 us (0.930)
  Pallas kernels: 73.5 us -> 67.8 us
    pallas_call x1, Pallas kernels: 71.8 us -> 66 us  [per_device(): pl.pallas_call(kernel, out_shape=jax.ShapeDtypeStruct((6,) + block, F32),...]
where the time goes in v3:
time: 69.4 us; the launch traced here: 68.4 us
  Pallas kernels  67.8 us (98%)
    pallas_call x1, Pallas kernels, per_device(): pl.pallas_call(kernel, out_shape=jax.ShapeDtypeStruct((6,) + block, F32),...  66 us
    pallas_call x1, Pallas kernels, per_device(): pl.pallas_call(write_out, out_shape=outs, in_specs=[vmem], out_specs=[hbm...  1.78 us

profile of v3, /device:TPU:1, one launch (start us, length us, event | category | flops | bytes accessed | tf_op | source)
XLA Modules:
  0.0 68.4 jit_solution(17636561687633138496)
XLA Ops:
  0.6 66.0 %shard_map.145.all_ref = f32[6,128,128]{2,1,0:T(8,128)} custom-call(bf16[1,128,512]{2,1,0:T(8,128)(2,1)} %x_ref.1, bf16[1,128,512]{2,1,0:T(8,128)(2,1)} %d_ref.1, bf16[1,128,128]{2,1,0:T(8,128)(2,1)} %wg_ref.1, bf16[1,128,128]{2,1,0:T(8,128)(2,1)} %wu_ref.1, bf16[1,128,128]{2,1,0:T(8,128)(2,1)} %wd_ref.1, f32[1,1,128,128]{3,2,1,0:T(8,128)} %mg_ref.1, ...), custom_call_target="tpu_custom_call" | custom-call | flops 1700000000 | bytes 2000000 | tf_op jit(solution)/shard_map/pallas_call | solution.py:434
  66.6 1.8 %shard_map.146 = (f32[1,1,128,128]{3,2,1,0:T(8,128)}, f32[1,1,128,128]{3,2,1,0:T(8,128)}, f32[1,1,128,128]{3,2,1,0:T(8,128)}, f32[1,128,128]{2,1,0:T(8,128)}, f3...) custom-call(f32[6,128,128]{2,1,0:T(8,128)} %shard_map.145.all_ref), custom_call_target="tpu_custom_call" | custom-call | tf_op jit(solution)/shard_map/pallas_call | solution.py:449

commit v4 on v3

--- a/solution.py
+++ b/solution.py
@@ -207,14 +207,13 @@
         from_partner[i].wait_recv()
         pass_near[i].start()
 
-    for i in range(3):
+    for i in range(4):
         tokens_in(i)
-    w1_arrived(first)
-    tokens_in(3)
     on_sib.start()
     to_up.wait_recv()
     to_down.wait_recv()
     near_sib.start()
+    w1_arrived(first)
     w1_arrived(1 - first)
     for c, d in zip(pass_near, pass_far):
         c.wait_recv()
@@ -253,7 +252,7 @@
     def turn_of(ahead, half):
         up_turn = 4 - half - ahead
         down_turn = ahead - 5 + half
-        return jnp.where(ahead == 0, 4, jnp.where(ahead < 4, up_turn, jnp.where(ahead == 4, 0, down_turn)))
+        return jnp.where(ahead == 0, 2, jnp.where(ahead < 4, up_turn, jnp.where(ahead == 4, 0, down_turn)))
 
     def pass_on(kk, half, j):
         m = j // 2

time: 69.4 us -> 66.5 us (0.958); the launches traced: 68.4 us -> 66.3 us
  Pallas kernels: 67.8 us -> 65.7 us
    pallas_call x1, Pallas kernels: 66 us -> 63.9 us  [per_device(): pl.pallas_call(kernel, out_shape=jax.ShapeDtypeStruct((6,) + block, F32),...]
where the time goes in v4:
time: 66.5 us; the launch traced here: 66.3 us
  Pallas kernels  65.7 us (99%)
    pallas_call x1, Pallas kernels, per_device(): pl.pallas_call(kernel, out_shape=jax.ShapeDtypeStruct((6,) + block, F32),...  63.9 us
    pallas_call x1, Pallas kernels, per_device(): pl.pallas_call(write_out, out_shape=outs, in_specs=[vmem], out_specs=[hbm...  1.78 us

profile of v4, /device:TPU:1, one launch (start us, length us, event | category | flops | bytes accessed | tf_op | source)
XLA Modules:
  0.0 66.3 jit_solution(11297756637030225418)
XLA Ops:
  0.6 63.9 %shard_map.145.all_ref = f32[6,128,128]{2,1,0:T(8,128)} custom-call(bf16[1,128,512]{2,1,0:T(8,128)(2,1)} %x_ref.1, bf16[1,128,512]{2,1,0:T(8,128)(2,1)} %d_ref.1, bf16[1,128,128]{2,1,0:T(8,128)(2,1)} %wg_ref.1, bf16[1,128,128]{2,1,0:T(8,128)(2,1)} %wu_ref.1, bf16[1,128,128]{2,1,0:T(8,128)(2,1)} %wd_ref.1, f32[1,1,128,128]{3,2,1,0:T(8,128)} %mg_ref.1, ...), custom_call_target="tpu_custom_call" | custom-call | flops 1700000000 | bytes 2000000 | tf_op jit(solution)/shard_map/pallas_call | solution.py:433
  64.6 1.8 %shard_map.146 = (f32[1,1,128,128]{3,2,1,0:T(8,128)}, f32[1,1,128,128]{3,2,1,0:T(8,128)}, f32[1,1,128,128]{3,2,1,0:T(8,128)}, f32[1,128,128]{2,1,0:T(8,128)}, f3...) custom-call(f32[6,128,128]{2,1,0:T(8,128)} %shard_map.145.all_ref), custom_call_target="tpu_custom_call" | custom-call | tf_op jit(solution)/shard_map/pallas_call | solution.py:448

commit v5 on v4

--- a/solution.py
+++ b/solution.py
@@ -86,7 +86,7 @@
     kk_own = k_own // 4
     rb_own = f % 4
     skew = jnp.where(p_own == k_own % 2, 0, 1)
-    w1_to = [chip(z + hop + skew, h_own) for hop in (8, -6, 6, -4, 4, -2, 2, 0)]
+    w1_to = [chip(z + hop + skew, h_own) for hop in (8, 6, -6, 4, -4, 2, -2, 0)]
     w1_self = w1_to[-1] == f
 
     recv[...] = jnp.zeros(recv.shape, BF16)
@@ -176,7 +176,7 @@
     to_sib = tok_copy(14, slot, slot, SIDE, sib)
     on_sib = tok_copy(15, other, other, SIDE, sib)
     near_sib = tok_copy(16, slot + SIDE, slot + SIDE, SIDE, sib)
-    for c in to_partner + [to_up, to_down, to_sib]:
+    for c in to_partner + [to_sib]:
         c.start()
 
     def column_of(kk):
@@ -209,12 +209,14 @@
 
     for i in range(4):
         tokens_in(i)
+    to_up.start()
+    to_down.start()
     on_sib.start()
+    w1_arrived(first)
+    w1_arrived(1 - first)
     to_up.wait_recv()
     to_down.wait_recv()
     near_sib.start()
-    w1_arrived(first)
-    w1_arrived(1 - first)
     for c, d in zip(pass_near, pass_far):
         c.wait_recv()
         d.start()

time: 66.5 us -> 66.4 us (level)
  no operation moved by 1% of the time
where the time goes in v5:
time: 66.4 us; the launch traced here: 66.2 us
  Pallas kernels  65.6 us (99%)
    pallas_call x1, Pallas kernels, per_device(): pl.pallas_call(kernel, out_shape=jax.ShapeDtypeStruct((6,) + block, F32),...  63.8 us
    pallas_call x1, Pallas kernels, per_device(): pl.pallas_call(write_out, out_shape=outs, in_specs=[vmem], out_specs=[hbm...  1.78 us

profile of v5, /device:TPU:1, one launch (start us, length us, event | category | flops | bytes accessed | tf_op | source)
XLA Modules:
  0.0 66.2 jit_solution(7051811024942371992)
XLA Ops:
  0.6 63.8 %shard_map.145.all_ref = f32[6,128,128]{2,1,0:T(8,128)} custom-call(bf16[1,128,512]{2,1,0:T(8,128)(2,1)} %x_ref.1, bf16[1,128,512]{2,1,0:T(8,128)(2,1)} %d_ref.1, bf16[1,128,128]{2,1,0:T(8,128)(2,1)} %wg_ref.1, bf16[1,128,128]{2,1,0:T(8,128)(2,1)} %wu_ref.1, bf16[1,128,128]{2,1,0:T(8,128)(2,1)} %wd_ref.1, f32[1,1,128,128]{3,2,1,0:T(8,128)} %mg_ref.1, ...), custom_call_target="tpu_custom_call" | custom-call | flops 1700000000 | bytes 2000000 | tf_op jit(solution)/shard_map/pallas_call | solution.py:435
  64.5 1.8 %shard_map.146 = (f32[1,1,128,128]{3,2,1,0:T(8,128)}, f32[1,1,128,128]{3,2,1,0:T(8,128)}, f32[1,1,128,128]{3,2,1,0:T(8,128)}, f32[1,128,128]{2,1,0:T(8,128)}, f3...) custom-call(f32[6,128,128]{2,1,0:T(8,128)} %shard_map.145.all_ref), custom_call_target="tpu_custom_call" | custom-call | tf_op jit(solution)/shard_map/pallas_call | solution.py:450

commit v6 on v4

--- a/solution.py
+++ b/solution.py
@@ -86,7 +86,7 @@
     kk_own = k_own // 4
     rb_own = f % 4
     skew = jnp.where(p_own == k_own % 2, 0, 1)
-    w1_to = [chip(z + hop + skew, h_own) for hop in (8, -6, 6, -4, 4, -2, 2, 0)]
+    w1_to = [chip(z + hop + skew, h_own) for hop in (8, 6, -6, 4, -4, 2, -2, 0)]
     w1_self = w1_to[-1] == f
 
     recv[...] = jnp.zeros(recv.shape, BF16)

time: 66.5 us -> 66.5 us (level)
  no operation moved by 1% of the time
where the time goes in v6:
time: 66.5 us; the launch traced here: 66.3 us
  Pallas kernels  65.7 us (99%)
    pallas_call x1, Pallas kernels, per_device(): pl.pallas_call(kernel, out_shape=jax.ShapeDtypeStruct((6,) + block, F32),...  63.9 us
    pallas_call x1, Pallas kernels, per_device(): pl.pallas_call(write_out, out_shape=outs, in_specs=[vmem], out_specs=[hbm...  1.78 us

profile of v6, /device:TPU:1, one launch (start us, length us, event | category | flops | bytes accessed | tf_op | source)
XLA Modules:
  0.0 66.3 jit_solution(2732025844800856708)
XLA Ops:
  0.6 63.9 %shard_map.145.all_ref = f32[6,128,128]{2,1,0:T(8,128)} custom-call(bf16[1,128,512]{2,1,0:T(8,128)(2,1)} %x_ref.1, bf16[1,128,512]{2,1,0:T(8,128)(2,1)} %d_ref.1, bf16[1,128,128]{2,1,0:T(8,128)(2,1)} %wg_ref.1, bf16[1,128,128]{2,1,0:T(8,128)(2,1)} %wu_ref.1, bf16[1,128,128]{2,1,0:T(8,128)(2,1)} %wd_ref.1, f32[1,1,128,128]{3,2,1,0:T(8,128)} %mg_ref.1, ...), custom_call_target="tpu_custom_call" | custom-call | flops 1700000000 | bytes 2000000 | tf_op jit(solution)/shard_map/pallas_call | solution.py:433
  64.5 1.8 %shard_map.146 = (f32[1,1,128,128]{3,2,1,0:T(8,128)}, f32[1,1,128,128]{3,2,1,0:T(8,128)}, f32[1,1,128,128]{3,2,1,0:T(8,128)}, f32[1,128,128]{2,1,0:T(8,128)}, f3...) custom-call(f32[6,128,128]{2,1,0:T(8,128)} %shard_map.145.all_ref), custom_call_target="tpu_custom_call" | custom-call | tf_op jit(solution)/shard_map/pallas_call | solution.py:448
